TPU v7x, 128 devices: a whole 4x4x4 slice. The times are simulated.
128 devices in a mesh: pipe: 16 (over y_lo, x, core), tensor: 8 (over y_hi, z).
Axes of the slice: x: 4, y: 4 (y_hi: 2, y_lo: 2; y = y_hi * 2 + y_lo), z: 4, core: 2. Of those that a mesh axis runs over, the one named last changes fastest.
Arguments:
- stream: bfloat16 [16, 256, 12288], P('pipe', None, 'tensor'), may hold values from -6 to 6
- entering: bfloat16 [1, 256, 12288], P(None, None, 'tensor'), may hold values from -6 to 6
- gains: float32 [16, 12288], P('pipe'), may hold values from 0.1 to 1.9
- keys: bfloat16 [2, 16, 256, 6144], P(None, 'pipe', None, 'tensor')
- values: bfloat16 [2, 16, 256, 6144], P(None, 'pipe', None, 'tensor'), may hold values from -6 to 6
- out_weight: bfloat16 [16, 6144, 12288], P('pipe', 'tensor'), may hold values from -0.078125 to 0.078125
Outputs:
- outputs: bfloat16 [2, 16, 256, 12288], P(None, 'pipe', None, 'tensor')
All inputs are finite; a program needn't handle non-finite values.
Results may differ from a plain program's by a relative error of at most 0.04.
Values may be sent and summed in bfloat16 or wider, within the bound.
A program may use at most 128 MiB of HBM per device.

v0:
```python
import jax
import jax.numpy as jnp
from jax import lax
from jax.sharding import PartitionSpec as P

HEAD_DIM = 128


def from_behind(x, axis, by):
    length = lax.axis_size(axis)
    pairs = [(i, i + by) for i in range(length) if 0 <= i + by < length]
    return lax.ppermute(x, axis, pairs)


def attend_queries(queries, key_rows, value_rows, weight):
    rows = queries.shape[0]
    width = key_rows.shape[1]
    heads = width // HEAD_DIM
    query_heads = queries.reshape(rows, heads, HEAD_DIM)
    key_heads = key_rows.reshape(rows, heads, HEAD_DIM)
    value_heads = value_rows.reshape(rows, heads, HEAD_DIM)
    scores = jnp.einsum("thd,uhd->htu", query_heads, key_heads, preferred_element_type=jnp.float32)
    scores = scores / jnp.sqrt(jnp.float32(HEAD_DIM))
    rows_at = jnp.arange(rows, dtype=jnp.int32)
    causal = rows_at[None, :, None] >= rows_at[None, None, :]
    scores = jnp.where(causal, scores, jnp.float32(-1e30))
    top = jnp.max(scores, axis=2, keepdims=True)
    expo = jnp.exp(scores - top)
    probs = (expo / jnp.sum(expo, axis=2, keepdims=True)).astype(jnp.bfloat16)
    context = jnp.einsum("htu,uhd->thd", probs, value_heads, preferred_element_type=jnp.float32)
    context = context.astype(jnp.bfloat16).reshape(rows, width)
    return jnp.dot(context, weight, preferred_element_type=jnp.float32)


def attend(whole, gain, key_rows, value_rows, weight, rank):
    width = key_rows.shape[1]
    xf = whole.astype(jnp.float32)
    center = jnp.mean(xf, axis=1, keepdims=True)
    spread = jnp.mean((xf - center) * (xf - center), axis=1, keepdims=True)
    normed = ((xf - center) * lax.rsqrt(spread + 1e-05) * gain[None, :]).astype(jnp.bfloat16)
    queries = lax.dynamic_slice_in_dim(normed, rank * width, width, 1)
    return attend_queries(queries, key_rows, value_rows, weight)


def body(stream, entering, gains, keys, values, out_weight):
    rank = lax.axis_index("tensor")
    section = lax.axis_index("pipe")
    ticks = keys.shape[0]
    results = []
    piece = stream[0]
    for tick in range(ticks):
        whole = lax.all_gather(piece, "tensor", axis=1, tiled=True)
        term = attend(whole, gains[0], keys[tick, 0], values[tick, 0], out_weight[0], rank)
        summed = lax.psum_scatter(
            term.astype(jnp.bfloat16), "tensor", scatter_dimension=1, tiled=True
        ).astype(jnp.float32)
        result = (piece.astype(jnp.float32) + summed).astype(jnp.bfloat16)
        results.append(result)
        if tick + 1 < ticks:
            moved = from_behind(result, "pipe", 1)
            piece = jnp.where(section == 0, entering[tick], moved)
    return jnp.stack(results)[:, None]


def solution(mesh):
    in_specs = (
        P("pipe", None, "tensor"),
        P(None, None, "tensor"),
        P("pipe", None),
        P(None, "pipe", None, "tensor"),
        P(None, "pipe", None, "tensor"),
        P("pipe", "tensor", None),
    )
    out_specs = P(None, "pipe", None, "tensor")
    return jax.shard_map(body, mesh=mesh, in_specs=in_specs, out_specs=out_specs, check_vma=False)
```

profile of v0, /device:TPU:0, one launch (start us, length us, event | category | flops | bytes accessed | tf_op | source)
XLA Modules:
  0.0 452.8 jit_solution(5238400309487397898)
XLA Ops:
  7.3 1.9 fusion.29
  9.4 0.8 fusion.30
  10.2 0.9 copy.16
  11.1 0.8 dynamic-slice
  11.9 89.3 %all-gather.6.cloned.1.call-done = bf16[1,256,12288]{2,1,0:T(8,128)(2,1)} async-done(((bf16[1,256,1536]{2,1,0:T(8,128)(2,1)}), bf16[1,256,12288]{2,1,0:T(8,128)(2,1)}) %all-gather.6.cloned.1.call-update) | async-done | bytes 6291472 | tf_op jit(solution)/shard_map/all_gather | solution.py:52
  101.2 3.9 convert_reduce_fusion
  105.1 0.7 copy-done
  105.8 3.2 multiply_reduce_fusion.1
  109.4 0.7 fusion.31
  110.7 13.6 %fusion.6 = bf16[256,12288]{1,0:T(8,128)(2,1)} fusion(bf16[256,768]{0,1:T(8,128)(2,1)S(1)} %bitcast.55, bf16[1,768,12288]{2,1,0:T(8,128)(2,1)} %param.11), kind=kOutput, calls=%fused_computation.10 | convolution fusion | flops 4834983936 | bytes 25559040 | tf_op jit(solution)/shard_map/dot_general | solution.py:32
  124.4 96.3 %reduce-scatter.3.cloned.1.call-done = bf16[256,1536]{1,0:T(8,128)(2,1)} async-done(((bf16[256,12288]{1,0:T(8,128)(2,1)}), bf16[256,1536]{1,0:T(8,128)(2,1)}) %reduce-scatter.3.cloned.1.call-update) | async-done | bytes 786448 | tf_op jit(solution)/shard_map/reduce_scatter | solution.py:54
  220.7 1.3 fusion.15
  222.0 1.3 collective-permute-start
  223.4 1.8 collective-permute-done
  225.2 1.0 bitcast_select_fusion
  226.5 0.9 copy.32
  227.6 96.2 %all-gather.4.cloned.1.call-done = bf16[256,12288]{1,0:T(8,128)(2,1)} async-done(((bf16[256,1536]{1,0:T(8,128)(2,1)}), bf16[256,12288]{1,0:T(8,128)(2,1)}) %all-gather.4.cloned.1.call-update) | async-done | bytes 6291472 | tf_op jit(solution)/shard_map/all_gather | solution.py:52
  323.8 3.9 convert_reduce_fusion.1
  328.4 3.2 multiply_reduce_fusion
  332.6 0.7 fusion.32
  333.6 13.6 %fusion.9 = bf16[256,12288]{1,0:T(8,128)(2,1)} fusion(bf16[256,768]{0,1:T(8,128)(2,1)S(1)} %bitcast.56, bf16[1,768,12288]{2,1,0:T(8,128)(2,1)} %param.11), kind=kOutput, calls=%fused_computation.11 | convolution fusion | flops 4834983936 | bytes 25559040 | tf_op jit(solution)/shard_map/dot_general | solution.py:32
  347.2 96.5 %reduce-scatter.5.cloned.1.call-done = bf16[256,1536]{1,0:T(8,128)(2,1)} async-done(((bf16[256,12288]{1,0:T(8,128)(2,1)}), bf16[256,1536]{1,0:T(8,128)(2,1)}) %reduce-scatter.5.cloned.1.call-update) | async-done | bytes 786448 | tf_op jit(solution)/shard_map/reduce_scatter | solution.py:54
  443.7 1.3 fusion.18
  445.0 1.3 maximum_bitcast_fusion
  (44 shorter events, 4.3 us)
Async XLA Ops:
  6.5 2.9 copy-start.9
  6.5 94.7 %all-gather.6.cloned.1.call-start = ((), (), s32[]{:S(2)}) async-start(), calls=%async_computation.5 | async-start | bytes 7077888 | tf_op jit(solution)/shard_map/all_gather | solution.py:52
  7.3 213.4 %reduce-scatter.3.cloned.1.call-start = ((), (), s32[]{:S(2)}) async-start(), calls=%async_computation.2 | async-start | bytes 7077888 | tf_op jit(solution)/shard_map/reduce_scatter | solution.py:54
  101.2 4.6 %copy-start = (bf16[1,256,12288]{2,1,0:T(8,128)(2,1)S(1)}, bf16[1,256,12288]{2,1,0:T(8,128)(2,1)}, u32[]{:S(2)}) copy-start(bf16[1,256,12288]{2,1,0:T(8,128)(2,1)} %all-gather.6.cloned.1.call-done) | copy-start | bytes 18874372
  109.4 1.0 copy-start.10
  124.3 96.4 %copy-start.3 = (bf16[1,256,1536]{2,1,0:T(8,128)(2,1)S(1)}, bf16[1,256,1536]{2,1,0:T(8,128)(2,1)}, u32[]{:S(2)}) copy-start(bf16[1,256,1536]{2,1,0:T(8,128)(2,1)} %param.6) | copy-start | bytes 2359300
  124.3 100.9 %copy-start.8 = (bf16[1,256,1536]{2,1,0:T(8,128)(2,1)S(1)}, bf16[1,256,1536]{2,1,0:T(8,128)(2,1)}, u32[]{:S(2)}) copy-start(bf16[1,256,1536]{2,1,0:T(8,128)(2,1)} %param.7) | copy-start | bytes 2359300
  124.3 199.5 %all-gather.4.cloned.1.call-start = ((), (), s32[]{:S(2)}) async-start(), calls=%async_computation.3 | async-start | bytes 7077888 | tf_op jit(solution)/shard_map/all_gather | solution.py:52
  222.0 4.2 copy-start.4
  222.0 3.2 collective-permute-start
  223.4 3.1 copy-start.6
  223.4 4.0 copy-start.7
  226.2 217.5 %reduce-scatter.5.cloned.1.call-start = ((), (), s32[]{:S(2)}) async-start(), calls=%async_computation.4 | async-start | bytes 7077888 | tf_op jit(solution)/shard_map/reduce_scatter | solution.py:54
  323.8 4.6 %copy-start.1 = (bf16[256,12288]{1,0:T(8,128)(2,1)S(1)}, bf16[256,12288]{1,0:T(8,128)(2,1)}, u32[]{:S(2)}) copy-start(bf16[256,12288]{1,0:T(8,128)(2,1)} %all-gather.4.cloned.1.call-done) | copy-start | bytes 18874372
  331.6 1.0 copy-start.11
  347.2 96.5 %copy-start.2 = (bf16[256,1536]{1,0:T(8,128)(2,1)S(1)}, bf16[256,1536]{1,0:T(8,128)(2,1)}, u32[]{:S(2)}) copy-start(bf16[256,1536]{1,0:T(8,128)(2,1)} %bitcast_select_fusion) | copy-start | bytes 2359300
  347.2 97.8 %copy-start.5 = (bf16[256,1536]{1,0:T(8,128)(2,1)S(1)}, bf16[256,1536]{1,0:T(8,128)(2,1)}, u32[]{:S(2)}) copy-start(bf16[256,1536]{1,0:T(8,128)(2,1)} %copy-done.4) | copy-start | bytes 2359300
Sparse Core Ops, SparseCore 0:
  9.7 91.5 all-gather.5
  124.4 96.2 reduce-scatter.2
  226.3 97.3 all-gather.3
  347.4 96.2 reduce-scatter.4
where the time goes:
time: 453 us
  waiting for transfers between devices  381 us (84%)
  matrix products  29.2 us (6%)
  other arithmetic  19.4 us (4%)
  between operations  13.3 us (3%)
  local copies, waits for them, and re-layouts  8.39 us (2%)
    reduce_scatter x2, waiting for transfers between devices, body(): lax.psum_scatter(term.astype(jnp.bfloat16), 'tensor', scatter_dimension=1...  193 us
    all_gather x2, waiting for transfers between devices, body(): whole = lax.all_gather(piece, 'tensor', axis=1, tiled=True)  186 us
    dot_general x2, matrix products, attend_queries(): return jnp.dot(context, weight, preferred_element_type=jnp.float32)  27.2 us
  transfers between devices with their start and end apart: 5, of which 5 were waited for; matrix products, arithmetic and copies ran while one was open for 1% of the time, Pallas kernels for 0%

commit v1 on v0

v1 whole, which is shorter than its diff:
```python
import functools

import jax
import jax.numpy as jnp
from jax import lax
from jax.experimental import pallas as pl
from jax.experimental.pallas import tpu as pltpu
from jax.sharding import PartitionSpec as P

HEAD_DIM = 128
ROWS = 64
MESH = pl.DeviceIdType.MESH
F32 = jnp.float32
BF16 = jnp.bfloat16

A, B, Y = 1, 3, 4
ORDERS = ((A, B, Y), (B, Y, A), (Y, A, B))
N_ORDERS = 3
N_SENT = 7


def flipped(rank, mask):
    y, z = rank // 4, rank % 4
    low = mask % 4
    if low == 1:
        z = z + 1 - 2 * (z % 2)
    elif low == 2:
        z = (z + 2) % 4
    elif low == 3:
        z = 3 - z
    if mask >= 4:
        y = 1 - y
    return y * 4 + z


def held_masks(order):
    first, second, third = ORDERS[order]
    return (
        first ^ second ^ third,
        first ^ second,
        first ^ third,
        first,
        second ^ third,
        second,
        third,
        0,
    )


def centred(block):
    total = jnp.sum(block, axis=1, keepdims=True)
    off = block - total / block.shape[1]
    return total, jnp.sum(off * off, axis=1, keepdims=True)


def as_rows(total, squares):
    rows = total.shape[0]
    lane = lax.broadcasted_iota(jnp.int32, (rows, 128), 1)
    both = jnp.where(lane == 0, total, jnp.where(lane == 1, squares, 0.0))
    if rows < 128:
        both = jnp.concatenate([both, jnp.zeros((128 - rows, 128), F32)], axis=0)
    return both.T[0:8]


def kernel(
    sizes, stream, entering, gains, keys, values, weight, out,
    w_held, k_held, v_held, x_held, q_held, gain_held, enter_held, ctx, sent, got, result, relay, stat_mine, stat_all,
    w_sem, load_sem, got_sem, sent_sem, stat_sem, stat_sent, q_sem, q_sent, x_sem, x_sent, out_sem,
):
    n_pipe, ticks, tokens, width, piece = sizes
    rows = ROWS
    chunks = tokens // rows
    units = ticks * chunks
    third = piece // N_ORDERS
    heads = width // HEAD_DIM
    features = piece * 8
    section, rank = lax.axis_index("pipe"), lax.axis_index("tensor")
    after, before = (section + 1) % n_pipe, (section + n_pipe - 1) % n_pipe

    x_load = pltpu.make_async_copy(stream.at[0], x_held.at[0], load_sem.at[0])
    x_load.start()
    w_loads = []
    loads = [
        pltpu.make_async_copy(
            gains.at[:, pl.ds(pl.multiple_of(rank * width, 128), width)], gain_held, load_sem.at[1]
        ),
        pltpu.make_async_copy(keys.at[:, 0], k_held, load_sem.at[2]),
        pltpu.make_async_copy(values.at[:, 0], v_held, load_sem.at[3]),
    ]
    for copy in loads:
        copy.start()
    for place in range(8):
        for order in range(N_ORDERS):
            owner = flipped(rank, held_masks(order)[place])
            start = pl.multiple_of(owner * piece + order * third, 128)
            copy = pltpu.make_async_copy(
                weight.at[0, :, pl.ds(start, third)],
                w_held.at[place * N_ORDERS + order],
                w_sem.at[place * N_ORDERS + order],
            )
            copy.start()
            w_loads.append(copy)
    enter_load = pltpu.make_async_copy(entering.at[0], enter_held, load_sem.at[4])
    enter_load.start()

    barrier = pltpu.get_barrier_semaphore()
    for peer in range(8):
        pl.semaphore_signal(barrier, inc=1, device_id=(before, peer), device_id_type=MESH)
    for mask in range(1, 8):
        pl.semaphore_signal(
            barrier, inc=1, device_id=(section, flipped(rank, mask)), device_id_type=MESH
        )
    pl.semaphore_wait(barrier, 15)

    def query_rows(chunk):
        return pl.ds(pl.multiple_of(chunk * rows, rows), rows)

    @pl.when(rank < 4)
    def _():
        for chunk in range(chunks):
            for half in range(2):
                source = stream.at[0, query_rows(chunk), pl.ds(half * width, width)]
                target = q_held.at[0, query_rows(chunk)]

                def far(source=source, target=target, half=half, chunk=chunk):
                    pltpu.make_async_remote_copy(
                        source, target, q_sent.at[0, half], q_sem.at[chunk],
                        device_id=(section, 2 * rank + half), device_id_type=MESH,
                    ).start()

                if half == 0:

                    @pl.when(rank == 0)
                    def _(source=source, target=target, chunk=chunk):
                        pltpu.make_async_copy(source, target, q_sem.at[chunk]).start()

                    pl.when(rank > 0)(far)
                else:
                    far()

    x_load.wait()
    for chunk in range(chunks):
        block = x_held[0, chunk * rows : (chunk + 1) * rows, :].astype(F32)
        line = as_rows(*centred(block))
        stat_mine[chunk] = line
        stat_all[rank, chunk] = line
    for mask in range(1, 8):
        pltpu.make_async_remote_copy(
            stat_mine.at[pl.ds(0, chunks)],
            stat_all.at[rank, pl.ds(0, chunks)],
            stat_sent.at[0],
            stat_sem.at[0, rank],
            device_id=(section, flipped(rank, mask)),
            device_id_type=MESH,
        ).start()
    for copy in loads:
        copy.wait()

    def hop(unit, slot, mask):
        return pltpu.make_async_remote_copy(
            sent.at[unit, slot],
            got.at[unit, slot],
            sent_sem.at[unit],
            got_sem.at[unit, slot],
            device_id=(section, flipped(rank, mask)),
            device_id_type=MESH,
        )

    def product(unit, place, order):
        return jnp.dot(
            ctx[unit], w_held[place * N_ORDERS + order], preferred_element_type=F32
        )

    def arrived(unit, slot):
        hop(unit, slot, A).wait_recv()
        return got[unit, slot].astype(F32)

    def have(unit, slot):
        return got[unit, slot].astype(F32)

    def slot_of(order, place):
        return place * N_ORDERS + order

    def attend(unit):
        tick, chunk = unit // chunks, unit % chunks
        at = query_rows(chunk)

        @pl.when(unit == 0)
        def _():
            for mask in range(1, 8):
                peer = flipped(rank, mask)
                pltpu.make_async_remote_copy(
                    stat_mine.at[pl.ds(0, chunks)], stat_all.at[peer, pl.ds(0, chunks)],
                    stat_sent.at[0], stat_sem.at[0, peer], device_id=(section, peer), device_id_type=MESH,
                ).wait_recv()

        @pl.when(tick > 0)
        def _():
            for peer in range(8):
                pltpu.make_async_remote_copy(
                    stat_mine.at[unit], stat_all.at[peer, unit],
                    stat_sent.at[1], stat_sem.at[1 + chunk, peer], device_id=(after, peer), device_id_type=MESH,
                ).wait_recv()

        pltpu.make_async_remote_copy(
            q_held.at[tick, at], q_held.at[tick, at], q_sent.at[0, 0], q_sem.at[unit],
            device_id=(after, rank), device_id_type=MESH,
        ).wait_recv()

        lines = [stat_all[peer, unit] for peer in range(8)]
        mean = sum(line[0:1] for line in lines) / features
        spread = sum(
            line[1:2] + (line[0:1] / piece - mean) * (line[0:1] / piece - mean) * piece
            for line in lines
        )
        scale = lax.rsqrt(spread / features + 1e-05)
        mean = jnp.broadcast_to(mean, (128, 128)).T[0:rows]
        scale = jnp.broadcast_to(scale, (128, 128)).T[0:rows]
        row = lax.broadcasted_iota(jnp.int32, (rows, tokens), 0) + chunk * rows
        column = lax.broadcasted_iota(jnp.int32, (rows, tokens), 1)
        causal = row >= column
        for head in range(heads):
            span = slice(head * HEAD_DIM, (head + 1) * HEAD_DIM)
            raw = q_held[tick, at, span].astype(F32)
            query = ((raw - mean) * scale * gain_held[0:1, span]).astype(BF16)
            scores = lax.dot_general(
                query, k_held[tick, :, span], (((1,), (1,)), ((), ())), preferred_element_type=F32
            )
            scores = jnp.where(causal, scores * (HEAD_DIM**-0.5), -1e30)
            expo = jnp.exp(scores - jnp.max(scores, axis=1, keepdims=True))
            probs = (expo * (1.0 / jnp.sum(expo, axis=1, keepdims=True))).astype(BF16)
            mixed = jnp.dot(probs, v_held[tick, :, span], preferred_element_type=F32)
            ctx[unit, :, span] = mixed.astype(BF16)

        for place in range(4):
            for order in range(N_ORDERS):

                @pl.when(unit == 0)
                def _(place=place, order=order):
                    w_loads[place * N_ORDERS + order].wait()

                slot = slot_of(order, place)
                sent[unit, slot] = product(unit, place, order).astype(BF16)
                hop(unit, slot, ORDERS[order][0]).start()

    def second(unit):
        for place in (4, 5):
            for order in range(N_ORDERS):

                @pl.when(unit == 0)
                def _(place=place, order=order):
                    w_loads[place * N_ORDERS + order].wait()

                slot = slot_of(order, place)
                value = product(unit, place, order) + arrived(unit, slot_of(order, place - 4))
                sent[unit, slot] = value.astype(BF16)
                hop(unit, slot, ORDERS[order][1]).start()

    def last(unit):
        for order in range(N_ORDERS):

            @pl.when(unit == 0)
            def _(order=order):
                w_loads[6 * N_ORDERS + order].wait()

            slot = slot_of(order, 6)
            value = product(unit, 6, order) + arrived(unit, slot_of(order, 2))
            value = value + arrived(unit, slot_of(order, 4))
            sent[unit, slot] = value.astype(BF16)
            hop(unit, slot, ORDERS[order][2]).start()

    def relay_x(chunk):
        return pltpu.make_async_remote_copy(
            relay.at[chunk], x_held.at[1, query_rows(chunk)], x_sent.at[0], x_sem.at[chunk],
            device_id=(after, rank), device_id_type=MESH,
        )

    def finish(unit):
        tick, chunk = unit // chunks, unit % chunks
        at = query_rows(chunk)

        @pl.when(unit == 0)
        def _():
            enter_load.wait()
            for order in range(N_ORDERS):
                w_loads[7 * N_ORDERS + order].wait()

        @pl.when(tick > 0)
        def _():
            relay_x(chunk).wait_recv()

        for order in range(N_ORDERS):
            span = slice(order * third, (order + 1) * third)
            value = product(unit, 7, order) + x_held[tick, at, span].astype(F32)
            for place in (3, 5, 6):
                value = value + arrived(unit, slot_of(order, place))
            result[unit, :, span] = value.astype(BF16)
        pltpu.make_async_copy(result.at[unit], out.at[tick, 0, at], out_sem.at[unit]).start()

        @pl.when(tick == 0)
        def _():
            @pl.when(section == n_pipe - 1)
            def _():
                relay[chunk] = enter_held[at]

            @pl.when(section < n_pipe - 1)
            def _():
                relay[chunk] = result[unit]

            stat_mine[chunks + chunk] = as_rows(*centred(relay[chunk].astype(F32)))
            for peer in range(8):
                pltpu.make_async_remote_copy(
                    stat_mine.at[chunks + chunk], stat_all.at[rank, chunks + chunk],
                    stat_sent.at[1], stat_sem.at[1 + chunk, rank], device_id=(after, peer), device_id_type=MESH,
                ).start()

            @pl.when(rank < 4)
            def _():
                for half in range(2):
                    pltpu.make_async_remote_copy(
                        relay.at[chunk, :, pl.ds(half * width, width)], q_held.at[1, at],
                        q_sent.at[1, half], q_sem.at[chunks + chunk],
                        device_id=(after, 2 * rank + half), device_id_type=MESH,
                    ).start()

            relay_x(chunk).start()

    def step(i, carry):
        pl.when(i < units)(lambda: attend(i))
        pl.when(i >= 3)(lambda: finish(i - 3))
        pl.when((i >= 2) & (i < units + 2))(lambda: last(i - 2))
        pl.when((i >= 1) & (i < units + 1))(lambda: second(i - 1))
        return carry

    lax.fori_loop(0, units + 3, step, 0)

    for unit in range(units):
        pltpu.make_async_remote_copy(
            sent.at[unit], got.at[unit], sent_sem.at[unit], got_sem.at[unit, 0],
            device_id=(section, flipped(rank, A)), device_id_type=MESH,
        ).wait_send()
        tick, chunk = divmod(unit, chunks)
        pltpu.make_async_copy(
            result.at[unit], out.at[tick, 0, query_rows(chunk)], out_sem.at[unit]
        ).wait()
    pltpu.make_async_remote_copy(
        stat_all.at[pl.ds(0, 7), pl.ds(0, chunks)], stat_all.at[pl.ds(0, 7), pl.ds(0, chunks)],
        stat_sent.at[0], stat_sem.at[0, 0], device_id=(after, rank), device_id_type=MESH,
    ).wait_send()
    pltpu.make_async_remote_copy(
        stat_all.at[:, pl.ds(0, chunks)], stat_all.at[:, pl.ds(0, chunks)],
        stat_sent.at[1], stat_sem.at[0, 0], device_id=(after, rank), device_id_type=MESH,
    ).wait_send()
    pltpu.make_async_remote_copy(
        x_held.at[1], x_held.at[1], x_sent.at[0], x_sem.at[0], device_id=(after, rank), device_id_type=MESH
    ).wait_send()

    def queries_sent(tick, half):
        pltpu.make_async_remote_copy(
            q_held.at[tick], q_held.at[tick], q_sent.at[tick, half], q_sem.at[0],
            device_id=(after, rank), device_id_type=MESH,
        ).wait_send()

    @pl.when(rank < 4)
    def _():
        pl.when(rank > 0)(lambda: queries_sent(0, 0))
        queries_sent(0, 1)
        queries_sent(1, 0)
        queries_sent(1, 1)


def body(n_pipe, stream, entering, gains, keys, values, weight):
    ticks, _, tokens, width = keys.shape
    piece = stream.shape[2]
    third = piece // N_ORDERS
    chunks = tokens // ROWS
    units = ticks * chunks
    vmem, dma = pltpu.VMEM, pltpu.SemaphoreType.DMA
    anywhere = pl.BlockSpec(memory_space=pl.ANY)
    return pl.pallas_call(
        functools.partial(kernel, (n_pipe, ticks, tokens, width, piece)),
        out_shape=jax.ShapeDtypeStruct((ticks, 1, tokens, piece), BF16),
        in_specs=[anywhere] * 6,
        out_specs=anywhere,
        scratch_shapes=[
            vmem((8 * N_ORDERS, width, third), BF16),
            vmem((ticks, tokens, width), BF16),
            vmem((ticks, tokens, width), BF16),
            vmem((ticks, tokens, piece), BF16),
            vmem((ticks, tokens, width), BF16),
            vmem((1, width), F32),
            vmem((tokens, piece), BF16),
            vmem((units, ROWS, width), BF16),
            vmem((units, N_SENT * N_ORDERS, ROWS, third), BF16),
            vmem((units, N_SENT * N_ORDERS, ROWS, third), BF16),
            vmem((units, ROWS, piece), BF16),
            vmem((chunks, ROWS, piece), BF16),
            vmem((units, 8, 128), F32),
            vmem((8, units, 8, 128), F32),
            dma((8 * N_ORDERS,)),
            dma((5,)),
            dma((units, N_SENT * N_ORDERS)),
            dma((units,)),
            dma((1 + chunks, 8)),
            dma((2,)),
            dma((units,)),
            dma((2, 2)),
            dma((chunks,)),
            dma((1,)),
            dma((units,)),
        ],
        compiler_params=pltpu.CompilerParams(
            collective_id=0, has_side_effects=True, vmem_limit_bytes=58 * 2**20
        ),
        name="relay",
    )(stream, entering, gains, keys, values, weight)


def solution(mesh):
    in_specs = (
        P("pipe", None, "tensor"),
        P(None, None, "tensor"),
        P("pipe", None),
        P(None, "pipe", None, "tensor"),
        P(None, "pipe", None, "tensor"),
        P("pipe", "tensor", None),
    )
    out_specs = P(None, "pipe", None, "tensor")
    return jax.shard_map(
        functools.partial(body, mesh.shape["pipe"]),
        mesh=mesh, in_specs=in_specs, out_specs=out_specs, check_vma=False,
    )
```

time: 453 us -> 141 us (0.31)
  waiting for transfers between devices: 381 us -> 0 us
  Pallas kernels: 0 us -> 138 us
  matrix products: 29.2 us -> 0 us
  other arithmetic: 19.4 us -> 0 us
  between operations: 13.3 us -> 0.01 us
  local copies, waits for them, and re-layouts: 8.39 us -> 2.65 us
    reduce_scatter x2 -> x0, waiting for transfers between devices: 193 us -> none  [body(): lax.psum_scatter(term.astype(jnp.bfloat16), 'tensor', scatter_dimension=1...]
    all_gather x2 -> x0, waiting for transfers between devices: 186 us -> none  [body(): whole = lax.all_gather(piece, 'tensor', axis=1, tiled=True)]
    pallas_call x0 -> x1, Pallas kernels: none -> 138 us  [body(): pl.pallas_call(functools.partial(kernel, (n_pipe, ticks, tokens, width, p...]
    dot_general x4 -> x0, matrix products: 27.8 us -> none  [the longest x2 27.2 us: attend_queries(): return jnp.dot(context, weight, preferred_element_type=jnp.float32)]
    reduce_sum x4 -> x0, other arithmetic: 14.2 us -> none  [the longest x2 7.75 us: attend(): center = jnp.mean(xf, axis=1, keepdims=True)]
  transfers between devices with their start and end apart: 5 -> 0, of which waited for: 5 -> 0; matrix products, arithmetic and copies ran while one was open for 1% -> 0% of each run, Pallas kernels for 0% -> 0%
where the time goes in v1:
time: 141 us
  Pallas kernels  138 us (98%)
  local copies, waits for them, and re-layouts  2.65 us (2%)
    pallas_call x1, Pallas kernels, body(): pl.pallas_call(functools.partial(kernel, (n_pipe, ticks, tokens, width, p...  138 us

profile of v1, /device:TPU:0, one launch (start us, length us, event | category | flops | bytes accessed | tf_op | source)
XLA Modules:
  0.0 141.1 jit_solution(2696144042707906703)
XLA Ops:
  0.0 138.5 %relay.1 = bf16[2,1,256,1536]{3,2,1,0:T(8,128)(2,1)} custom-call(bf16[1,256,1536]{2,1,0:T(8,128)(2,1)} %stream.1, bf16[1,256,1536]{2,1,0:T(8,128)(2,1)} %entering.1, f32[1,12288]{1,0:T(1,128)} %gains.1, bf16[2,1,256,768]{3,2,1,0:T(8,128)(2,1)} %keys.1, bf16[2,1,256,768]{3,2,1,0:T(8,128)(2,1)} %values.1, bf16[1,768,12288]{2,1,0:T(8,128)(2,1)} %weight.1), custom_call_target="tpu_custom_call" | custom-call | tf_op jit(solution)/shard_map/relay/pallas_call | solution.py:380
  138.5 2.7 %copy.8 = bf16[2,1,256,1536]{3,2,1,0:T(8,128)(2,1)} copy(bf16[2,1,256,1536]{3,2,1,0:T(8,128)(2,1)} %relay.1) | data formatting | bytes 3145728

commit v2 on v0

v2 whole, which is shorter than its diff:
```python
import functools

import jax
import jax.numpy as jnp
from jax import lax
from jax.experimental import pallas as pl
from jax.experimental.pallas import tpu as pltpu
from jax.sharding import PartitionSpec as P

HEAD_DIM = 128
PARTS = (64, 64, 128)
MESH = pl.DeviceIdType.MESH
F32 = jnp.float32
BF16 = jnp.bfloat16

A, B, Y = 1, 3, 4
ORDERS = ((A, B, Y), (B, Y, A), (Y, A, B))
N_ORDERS = 3
N_SENT = 7


def flipped(rank, mask):
    y, z = rank // 4, rank % 4
    low = mask % 4
    if low == 1:
        z = z + 1 - 2 * (z % 2)
    elif low == 2:
        z = (z + 2) % 4
    elif low == 3:
        z = 3 - z
    if mask >= 4:
        y = 1 - y
    return y * 4 + z


def held_masks(order):
    first, second, third = ORDERS[order]
    return (
        first ^ second ^ third,
        first ^ second,
        first ^ third,
        first,
        second ^ third,
        second,
        third,
        0,
    )


def centred(block):
    total = jnp.sum(block, axis=1, keepdims=True)
    off = block - total / block.shape[1]
    return total, jnp.sum(off * off, axis=1, keepdims=True)


def as_rows(total, squares):
    rows = total.shape[0]
    lane = lax.broadcasted_iota(jnp.int32, (rows, 128), 1)
    both = jnp.where(lane == 0, total, jnp.where(lane == 1, squares, 0.0))
    if rows < 128:
        both = jnp.concatenate([both, jnp.zeros((128 - rows, 128), F32)], axis=0)
    return both.T[0:8]


PLAN = (
    "a0", "p00", "p01", "w1", "p02", "p03", "s04", "s05", "a1", "w2", "p10", "p11", "l0", "p12", "p13", "f0",
    "a2", "p20", "s14", "s15", "p21", "x3", "p22", "p23", "w3", "l1", "f1", "s24", "s25", "a3", "p30", "t1",
    "p31", "x4", "l2", "p32", "p33", "w4", "f2", "a4", "p40", "p41", "s34", "s35", "t2", "p42", "p43", "x5",
    "s44", "s45", "l3", "w5", "a5", "p50", "p51", "l4", "p52", "p53", "f3", "s54", "s55", "f4", "l5", "f5",
)
ROUND = ((13, 1, 64), (15, 2, 128), (11, 2, 192))
ROUND_ROWS = 64


def kernel(
    sizes, stream, entering, gains, keys, values, weight, out,
    w_held, k_held, v_held, x_held, q_held, pass_held, gain_held, ctx, sent, got, turn_held, stat_mine, stat_all,
    w_sem, load_sem, got_sem, sent_sem, stat_sem, stat_sent, q_sem, q_sent, pass_sem, pass_sent, x_sem, x_sent, turn_sem, turn_sent,
):
    n_pipe, ticks, tokens, width, piece = sizes
    n = len(PARTS)
    first_row = [sum(PARTS[:i]) for i in range(n)]
    third = piece // N_ORDERS
    heads = width // HEAD_DIM
    features = piece * 8
    section, rank = lax.axis_index("pipe"), lax.axis_index("tensor")
    after, before = (section + 1) % n_pipe, (section + n_pipe - 1) % n_pipe

    def span_of(part):
        return pl.ds(first_row[part], PARTS[part])

    def both_of(unit):
        tick, part = divmod(unit, n)
        return pl.ds(tick * tokens + first_row[part], PARTS[part])

    def remote(source, target, send, receive, where):
        return pltpu.make_async_remote_copy(
            source, target, send, receive, device_id=where, device_id_type=MESH
        )

    barrier = pltpu.get_barrier_semaphore()
    for mask in range(1, 8):
        pl.semaphore_signal(
            barrier, inc=1, device_id=(section, flipped(rank, mask)), device_id_type=MESH
        )
    pl.semaphore_signal(barrier, inc=1, device_id=(before, rank), device_id_type=MESH)
    for turn, _, _ in ROUND:

        @pl.when(section == turn)
        def _():
            pl.semaphore_signal(barrier, inc=1, device_id=(7, rank), device_id_type=MESH)

        @pl.when(section == 8)
        def _(turn=turn):
            pl.semaphore_signal(barrier, inc=1, device_id=(turn, rank), device_id_type=MESH)


    x_load = pltpu.make_async_copy(stream.at[0], x_held.at[0], load_sem.at[0])
    x_load.start()
    w_loads = []
    loads = [
        pltpu.make_async_copy(
            gains.at[:, pl.ds(pl.multiple_of(rank * width, 128), width)], gain_held, load_sem.at[1]
        ),
        pltpu.make_async_copy(keys.at[:, 0], k_held, load_sem.at[2]),
        pltpu.make_async_copy(values.at[:, 0], v_held, load_sem.at[3]),
    ]
    for copy in loads:
        copy.start()
    for place in range(8):
        for order in range(N_ORDERS):
            owner = flipped(rank, held_masks(order)[place])
            start = pl.multiple_of(owner * piece + order * third, 128)
            w_loads.append(
                pltpu.make_async_copy(
                    weight.at[0, :, pl.ds(start, third)],
                    w_held.at[place * N_ORDERS + order],
                    w_sem.at[place * N_ORDERS + order],
                )
            )
    early = 2 * N_ORDERS
    for copy in w_loads[:early]:
        copy.start()

    enter_load = pltpu.make_async_copy(entering.at[0], x_held.at[1], load_sem.at[4])

    def query_send(tick, part, half):
        unit, at = tick * n + part, span_of(part)
        direct = tick == 0 and part == 0
        passed = (rank >= 2) if half == 0 else (rank == 2)
        target = 2 * rank + half
        source = x_held.at[tick, at, pl.ds(half * width, width)]

        def far():
            remote(
                source, q_held.at[tick, at], q_sent.at[tick, half], q_sem.at[unit], (section, target)
            ).start()

        def near():
            remote(
                source, pass_held.at[tick, at], q_sent.at[tick, half], pass_sem.at[unit], (section, target - 4)
            ).start()

        def own():
            pltpu.make_async_copy(source, q_held.at[tick, at], q_sem.at[unit]).start()

        away = (rank > 0) if half == 0 else (rank >= 0)
        if half == 0:
            pl.when(rank == 0)(own)
        if direct:
            pl.when(away)(far)
        else:
            pl.when(passed)(near)
            pl.when(away & (rank < 2) if half == 0 else (rank != 2))(far)

    def pass_on(unit):
        tick, part = divmod(unit, n)
        at = span_of(part)

        @pl.when(rank < 3)
        def _():
            copy = remote(
                pass_held.at[tick, at], pass_held.at[tick, at], q_sent.at[0, 0], pass_sem.at[unit], (after, rank)
            )
            copy.wait_recv()
            remote(
                pass_held.at[tick, at], q_held.at[tick, at], pass_sent.at[tick], q_sem.at[unit],
                (section, rank + 4),
            ).start()

    def measure(unit):
        tick, part = divmod(unit, n)
        line = as_rows(*centred(x_held[tick, span_of(part), :].astype(F32)))
        stat_mine[unit] = line
        stat_all[rank, unit] = line

    def distribute(unit):
        tick, part = divmod(unit, n)
        for mask in range(1, 8):
            remote(
                stat_mine.at[unit], stat_all.at[rank, unit], stat_sent.at[0], stat_sem.at[unit, rank],
                (section, flipped(rank, mask)),
            ).start()

        @pl.when(rank < 4)
        def _():
            for half in (1, 0):
                query_send(tick, part, half)

    def take(unit):
        part = unit - n
        if part == 0:
            pl.when(section == 0)(enter_load.wait)

        @pl.when(section > 0)
        def _():
            relay_x(part).wait_recv()

        measure(unit)
        distribute(unit)

    x_load.wait()
    for part in range(n):
        measure(part)
    helps = functools.reduce(lambda a, b: a | b, [section == turn for turn, _, _ in ROUND])

    @pl.when(section == 7)
    def _():
        pl.semaphore_wait(barrier, 8 + len(ROUND))

    @pl.when(helps)
    def _():
        pl.semaphore_wait(barrier, 9)

    @pl.when((section != 7) & jnp.logical_not(helps))
    def _():
        pl.semaphore_wait(barrier, 8)

    for part in range(n):
        distribute(part)

    for copy in w_loads[early:]:
        copy.start()
    pl.when(section == 0)(enter_load.start)
    for copy in loads:
        copy.wait()

    def hop(unit, slot, mask):
        at = both_of(unit)
        return remote(
            sent.at[slot, at], got.at[slot, at], sent_sem.at[slot], got_sem.at[unit, slot],
            (section, flipped(rank, mask)),
        )

    def product(unit, place, order):
        if unit == 0:
            w_loads[place * N_ORDERS + order].wait()
        return jnp.dot(
            ctx[both_of(unit), :], w_held[place * N_ORDERS + order], preferred_element_type=F32
        )

    def arrived(unit, slot):
        hop(unit, slot, A).wait_recv()
        return got[slot, both_of(unit), :].astype(F32)

    def slot_of(order, place):
        return place * N_ORDERS + order

    def attend(unit):
        tick, part = divmod(unit, n)
        rows = PARTS[part]
        for mask in range(1, 8):
            peer = flipped(rank, mask)
            remote(
                stat_mine.at[unit], stat_all.at[peer, unit], stat_sent.at[0], stat_sem.at[unit, peer],
                (section, peer),
            ).wait_recv()
        lines = [stat_all[peer, unit] for peer in range(8)]
        mean = sum(line[0:1] for line in lines) / features
        spread = sum(
            line[1:2] + (line[0:1] / piece - mean) * (line[0:1] / piece - mean) * piece
            for line in lines
        )
        scale = lax.rsqrt(spread / features + 1e-05)
        mean = jnp.broadcast_to(mean, (128, 128)).T[0:rows]
        scale = jnp.broadcast_to(scale, (128, 128)).T[0:rows]
        row = lax.broadcasted_iota(jnp.int32, (rows, tokens), 0) + first_row[part]
        column = lax.broadcasted_iota(jnp.int32, (rows, tokens), 1)
        causal = row >= column
        remote(
            q_held.at[tick, span_of(part)], q_held.at[tick, span_of(part)], q_sent.at[0, 0], q_sem.at[unit],
            (after, rank),
        ).wait_recv()
        spans = [slice(head * HEAD_DIM, (head + 1) * HEAD_DIM) for head in range(heads)]
        scores = []
        for span in spans:
            raw = q_held[tick, span_of(part), span].astype(F32)
            query = ((raw - mean) * scale * gain_held[0:1, span]).astype(BF16)
            scores.append(
                lax.dot_general(
                    query, k_held[tick, :, span], (((1,), (1,)), ((), ())), preferred_element_type=F32
                )
            )
        probs = []
        for score in scores:
            score = jnp.where(causal, score * (HEAD_DIM**-0.5), -1e30)
            expo = jnp.exp(score - jnp.max(score, axis=1, keepdims=True))
            probs.append((expo * (1.0 / jnp.sum(expo, axis=1, keepdims=True))).astype(BF16))
        mixed = [
            jnp.dot(prob, v_held[tick, :, span], preferred_element_type=F32).astype(BF16)
            for prob, span in zip(probs, spans)
        ]
        for value, span in zip(mixed, spans):
            ctx[both_of(unit), span] = value

    def send(unit, place, stage, values):
        for order in range(N_ORDERS):
            sent[slot_of(order, place), both_of(unit), :] = values[order].astype(BF16)
        for order in range(N_ORDERS):
            hop(unit, slot_of(order, place), ORDERS[order][stage]).start()

    def first(unit, place):
        send(unit, place, 0, [product(unit, place, order) for order in range(N_ORDERS)])

    def second(unit, place):
        values = [
            product(unit, place, order) + arrived(unit, slot_of(order, place - 4))
            for order in range(N_ORDERS)
        ]
        send(unit, place, 1, values)

    def last(unit):
        values = [
            product(unit, 6, order) + arrived(unit, slot_of(order, 2)) + arrived(unit, slot_of(order, 4))
            for order in range(N_ORDERS)
        ]
        send(unit, 6, 2, values)

    def relay_x(part):
        return remote(
            out.at[0, 0, span_of(part)], x_held.at[1, span_of(part)], x_sent.at[0], x_sem.at[part], (after, rank)
        )

    def turn_in(turn, row):
        return remote(
            out.at[0, 0, pl.ds(row, ROUND_ROWS)], turn_held, x_sent.at[0], turn_sem.at[0], (turn, rank)
        )

    def turn_out(part, row):
        return remote(
            turn_held, x_held.at[1, pl.ds(row, ROUND_ROWS)], turn_sent.at[0], x_sem.at[part], (8, rank)
        )

    def pass_turn(part):
        for turn, its_part, row in ROUND:
            if its_part == part:

                @pl.when(section == turn)
                def _(turn=turn, row=row):
                    turn_in(turn, row).wait_recv()
                    turn_out(part, row).start()

    def hand_over(part):
        turns = [entry for entry in ROUND if entry[1] == part]
        if not turns:
            pl.when(section < n_pipe - 1)(relay_x(part).start)
            return
        pl.when((section < n_pipe - 1) & (section != 7))(relay_x(part).start)

        @pl.when(section == 7)
        def _():
            for turn, _, row in turns:
                turn_in(turn, row).start()

    def finish(unit):
        tick, part = divmod(unit, n)
        at = span_of(part)
        values = []
        for order in range(N_ORDERS):
            span = slice(order * third, (order + 1) * third)
            value = product(unit, 7, order) + x_held[tick, at, span].astype(F32)
            for place in (3, 5, 6):
                value = value + arrived(unit, slot_of(order, place))
            values.append(value.astype(BF16))
        for order in range(N_ORDERS):
            out[tick, 0, at, order * third : (order + 1) * third] = values[order]
        if tick == 0:
            hand_over(part)

    work = {"x": take, "a": attend, "p": first, "s": second, "l": last, "f": finish, "w": pass_on, "t": pass_turn}
    for item in PLAN:
        work[item[0]](*(int(digit) for digit in item[1:]))

    for slot in range(N_SENT * N_ORDERS):
        remote(
            sent.at[slot], got.at[slot], sent_sem.at[slot], got_sem.at[0, 0], (section, flipped(rank, A))
        ).wait_send()
    some = stat_all.at[pl.ds(0, 7)]
    remote(some, some, stat_sent.at[0], stat_sem.at[0, 0], (after, rank)).wait_send()

    for turn, part, row in ROUND:
        pl.when(section == turn)(turn_out(part, row).wait_send)

    @pl.when(section < n_pipe - 1)
    def _():
        remote(x_held.at[1], x_held.at[1], x_sent.at[0], x_sem.at[0], (after, rank)).wait_send()

    def queries_sent(tick, half):
        remote(
            q_held.at[tick], q_held.at[tick], q_sent.at[tick, half], q_sem.at[0], (after, rank)
        ).wait_send()

    @pl.when(rank < 4)
    def _():
        for tick in range(ticks):
            pl.when(rank > 0)(functools.partial(queries_sent, tick, 0))
            queries_sent(tick, 1)

    @pl.when(rank < 3)
    def _():
        for tick in range(2):
            begun = pass_held.at[tick, pl.ds((1 - tick) * PARTS[0], tokens - (1 - tick) * PARTS[0])]
            remote(begun, begun, pass_sent.at[tick], pass_sem.at[0], (after, rank)).wait_send()


def body(n_pipe, stream, entering, gains, keys, values, weight):
    ticks, _, tokens, width = keys.shape
    piece = stream.shape[2]
    third = piece // N_ORDERS
    n = len(PARTS)
    slots = N_SENT * N_ORDERS
    vmem, dma = pltpu.VMEM, pltpu.SemaphoreType.DMA
    return pl.pallas_call(
        functools.partial(kernel, (n_pipe, ticks, tokens, width, piece)),
        out_shape=pltpu.VMEM((ticks, 1, tokens, piece), BF16),
        in_specs=[pl.BlockSpec(memory_space=pltpu.HBM)] * 6,
        out_specs=pl.BlockSpec(memory_space=pltpu.VMEM),
        scratch_shapes=[
            vmem((8 * N_ORDERS, width, third), BF16),
            vmem((ticks, tokens, width), BF16),
            vmem((ticks, tokens, width), BF16),
            vmem((ticks, tokens, piece), BF16),
            vmem((ticks, tokens, width), BF16),
            vmem((ticks, tokens, width), BF16),
            vmem((1, width), F32),
            vmem((ticks * tokens, width), BF16),
            vmem((slots, ticks * tokens, third), BF16),
            vmem((slots, ticks * tokens, third), BF16),
            vmem((ROUND_ROWS, piece), BF16),
            vmem((ticks * n, 8, 128), F32),
            vmem((8, ticks * n, 8, 128), F32),
            dma((8 * N_ORDERS,)),
            dma((5,)),
            dma((ticks * n, slots)),
            dma((slots,)),
            dma((ticks * n, 8)),
            dma((1,)),
            dma((ticks * n,)),
            dma((2, 2)),
            dma((ticks * n,)),
            dma((2,)),
            dma((n,)),
            dma((1,)),
            dma((1,)),
            dma((1,)),
        ],
        compiler_params=pltpu.CompilerParams(
            collective_id=0, has_side_effects=True, vmem_limit_bytes=52 * 2**20
        ),
        name="relay",
    )(stream, entering, gains, keys, values, weight)


def solution(mesh):
    in_specs = (
        P("pipe", None, "tensor"),
        P(None, None, "tensor"),
        P("pipe", None),
        P(None, "pipe", None, "tensor"),
        P(None, "pipe", None, "tensor"),
        P("pipe", "tensor", None),
    )
    out_specs = P(None, "pipe", None, "tensor")
    return jax.shard_map(
        functools.partial(body, mesh.shape["pipe"]),
        mesh=mesh, in_specs=in_specs, out_specs=out_specs, check_vma=False,
    )
```

time: 453 us -> 120 us (0.26)
  waiting for transfers between devices: 381 us -> 0 us
  Pallas kernels: 0 us -> 118 us
  matrix products: 29.2 us -> 0 us
  other arithmetic: 19.4 us -> 0 us
  between operations: 13.3 us -> 0.01 us
  local copies, waits for them, and re-layouts: 8.39 us -> 1.94 us
    reduce_scatter x2 -> x0, waiting for transfers between devices: 193 us -> none  [body(): lax.psum_scatter(term.astype(jnp.bfloat16), 'tensor', scatter_dimension=1...]
    all_gather x2 -> x0, waiting for transfers between devices: 186 us -> none  [body(): whole = lax.all_gather(piece, 'tensor', axis=1, tiled=True)]
    pallas_call x0 -> x1, Pallas kernels: none -> 118 us  [body(): pl.pallas_call(functools.partial(kernel, (n_pipe, ticks, tokens, width, p...]
    dot_general x4 -> x0, matrix products: 27.8 us -> none  [the longest x2 27.2 us: attend_queries(): return jnp.dot(context, weight, preferred_element_type=jnp.float32)]
    reduce_sum x4 -> x0, other arithmetic: 14.2 us -> none  [the longest x2 7.75 us: attend(): center = jnp.mean(xf, axis=1, keepdims=True)]
  transfers between devices with their start and end apart: 5 -> 0, of which waited for: 5 -> 0; matrix products, arithmetic and copies ran while one was open for 1% -> 0% of each run, Pallas kernels for 0% -> 0%
where the time goes in v2:
time: 120 us
  Pallas kernels  118 us (98%)
  local copies, waits for them, and re-layouts  1.94 us (2%)
    pallas_call x1, Pallas kernels, body(): pl.pallas_call(functools.partial(kernel, (n_pipe, ticks, tokens, width, p...  118 us

profile of v2, /device:TPU:0, one launch (start us, length us, event | category | flops | bytes accessed | tf_op | source)
XLA Modules:
  0.0 119.5 jit_solution(9337661273725945029)
XLA Ops:
  0.0 0.0 copy-start
  0.0 0.8 copy-done
  0.8 117.6 %relay.1 = bf16[2,1,256,1536]{3,2,1,0:T(8,128)(2,1)S(1)} custom-call(bf16[1,256,1536]{2,1,0:T(8,128)(2,1)} %stream.1, bf16[1,256,1536]{2,1,0:T(8,128)(2,1)} %entering.1, f32[1,12288]{1,0:T(1,128)S(1)} %copy-done, bf16[2,1,256,768]{3,2,1,0:T(8,128)(2,1)} %keys.1, bf16[2,1,256,768]{3,2,1,0:T(8,128)(2,1)} %values.1, bf16[1,768,12288]{2,1,0:T(8,128)(2,1)} %weight.1), custom_call_target="tpu_custom_call" | custom-call | tf_op jit(solution)/shard_map/relay/pallas_call | solution.py:433
  118.4 1.1 copy.8
Async XLA Ops:
  0.0 0.8 copy-start

commit v3 on v2

--- a/solution.py
+++ b/solution.py
@@ -465,7 +465,7 @@
             dma((1,)),
         ],
         compiler_params=pltpu.CompilerParams(
-            collective_id=0, has_side_effects=True, vmem_limit_bytes=52 * 2**20
+            collective_id=0, has_side_effects=True, vmem_limit_bytes=62 * 2**20 + 400 * 2**10
         ),
         name="relay",
     )(stream, entering, gains, keys, values, weight)

time: 120 us -> 119 us (level)
  no operation moved by 1% of the time
where the time goes in v3:
time: 119 us
  Pallas kernels  118 us (99%)
    pallas_call x1, Pallas kernels, body(): pl.pallas_call(functools.partial(kernel, (n_pipe, ticks, tokens, width, p...  118 us

profile of v3, /device:TPU:0, one launch (start us, length us, event | category | flops | bytes accessed | tf_op | source)
XLA Modules:
  0.0 118.8 jit_solution(12857359830945031781)
XLA Ops:
  0.0 117.7 %relay.1 = bf16[2,1,256,1536]{3,2,1,0:T(8,128)(2,1)S(1)} custom-call(bf16[1,256,1536]{2,1,0:T(8,128)(2,1)} %stream.1, bf16[1,256,1536]{2,1,0:T(8,128)(2,1)} %entering.1, f32[1,12288]{1,0:T(1,128)} %gains.1, bf16[2,1,256,768]{3,2,1,0:T(8,128)(2,1)} %keys.1, bf16[2,1,256,768]{3,2,1,0:T(8,128)(2,1)} %values.1, bf16[1,768,12288]{2,1,0:T(8,128)(2,1)} %weight.1), custom_call_target="tpu_custom_call" | custom-call | tf_op jit(solution)/shard_map/relay/pallas_call | solution.py:433
  117.7 1.1 copy.8
